TPU v7x, 256 devices: a whole 4x4x8 slice. The times are simulated.
256 devices in a mesh: tok: 2 (over core), row: 8 (over x, z_lo), col: 16 (over z_hi, y).
Axes of the slice: x: 4, y: 4, z: 8 (z_hi: 4, z_lo: 2; z = z_hi * 2 + z_lo), core: 2. Of those that a mesh axis runs over, the one named last changes fastest.
Arguments:
- tokens: bfloat16 [1024, 8192], P('tok', 'col'), may hold values from -6 to 6
- gate_weight: bfloat16 [8192, 16384], P(None, ('row', 'col')), may hold values from -0.0625 to 0.0625
- up_weight: bfloat16 [8192, 16384], P(None, ('row', 'col')), may hold values from -0.0625 to 0.0625
Outputs:
- gram: float32 [8, 16384, 16, 128], P('tok', 'row', 'col')
- panel: float32 [16384, 256], P(('row', 'col'), 'tok')
All inputs are finite; a program needn't handle non-finite values.
Results may differ from a plain program's by a relative error of at most 0.0046.
Values may be sent and summed in bfloat16 or wider, within the bound.
A program may use at most 64 MiB of HBM per device.

v0:
```python
import jax
import jax.numpy as jnp
from jax import lax
from jax.sharding import PartitionSpec as P

PANEL = 256


def spread(array, axis, root):
    mine = lax.axis_index(axis) == root
    return lax.psum(jnp.where(mine, array, jnp.zeros_like(array)), axis)


def local(tokens, gate_weight, up_weight):
    tok_rows = tokens.shape[0]
    width = gate_weight.shape[1]
    piece = lax.all_gather(tokens, "col", axis=1, tiled=True)
    gate = jnp.dot(piece, gate_weight, preferred_element_type=jnp.float32)
    up = jnp.dot(piece, up_weight, preferred_element_type=jnp.float32)
    hidden = (jax.nn.silu(gate) * up).astype(jnp.bfloat16)
    n_row = lax.axis_size("row")
    n_tok = lax.axis_size("tok")
    half = n_row // n_tok
    row_block = lax.all_gather(hidden, "col", axis=1, tiled=True)
    col_group = lax.all_gather(hidden, "row", axis=1, tiled=True).reshape(tok_rows, n_row, width)
    mine = lax.psum_scatter(
        jnp.einsum("ti,tak->aik", row_block, col_group, preferred_element_type=jnp.float32),
        "tok",
        scatter_dimension=0,
        tiled=True,
    )
    gram_tile = mine.reshape(half, mine.shape[1], 1, width)
    leading = mine[0]
    blocks = max(PANEL // width, 1)
    pieces = []
    for root in range(blocks):
        pieces.append(spread(leading, ("tok", "col"), root))
    columns = jnp.concatenate(pieces, axis=1)
    corner = spread(columns[:PANEL], "row", 0)
    own_rows = lax.dynamic_slice_in_dim(columns, lax.axis_index("col") * width, width, 0)
    factor = jnp.linalg.cholesky(corner)
    solved = lax.linalg.triangular_solve(
        factor, own_rows, left_side=False, lower=True, transpose_a=True
    )
    share = PANEL // n_tok
    panel = lax.dynamic_slice_in_dim(solved, lax.axis_index("tok") * share, share, 1)
    return (gram_tile, panel)


def solution(mesh):
    placed = (P("tok", "col"), P(None, ("row", "col")), P(None, ("row", "col")))
    return jax.shard_map(
        local,
        mesh=mesh,
        in_specs=placed,
        out_specs=(P("tok", "row", "col", None), P(("row", "col"), "tok")),
        check_vma=False,
    )
```

profile of v0, /device:TPU:27, one launch (start us, length us, event | category | flops | bytes accessed | tf_op | source)
XLA Modules:
  0.0 754.4 jit_solution(11648126967606940137)
XLA Ops:
  7.2 0.7 all-gather.4.cloned.1.call-update
  8.0 129.5 %all-gather.4.cloned.1.call-done = bf16[512,8192]{1,0:T(8,128)(2,1)} async-done(((bf16[512,512]{1,0:T(8,128)(2,1)}), bf16[512,8192]{1,0:T(8,128)(2,1)}) %all-gather.4.cloned.1.call-update) | async-done | bytes 8388624 | tf_op jit(solution)/shard_map/all_gather | solution.py:17
  137.5 5.9 fusion.13
  143.3 0.5 copy-done.4
  143.8 3.0 fusion.1
  146.8 0.0 all-gather.8.cloned.1.call-start
  146.9 0.7 all-gather.8.cloned.1.call-update
  147.6 35.6 %all-gather.6.cloned.1.call-done = bf16[512,1024]{1,0:T(8,128)(2,1)} async-done(((bf16[512,128]{1,0:T(8,128)(2,1)}), bf16[512,1024]{1,0:T(8,128)(2,1)}) %all-gather.6.cloned.1.call-update) | async-done | bytes 1048592 | tf_op jit(solution)/shard_map/all_gather | solution.py:25
  183.3 1.5 copy.13
  184.8 69.9 %all-gather.8.cloned.1.call-done = bf16[512,2048]{1,0:T(8,128)(2,1)} async-done(((bf16[512,128]{1,0:T(8,128)(2,1)}), bf16[512,2048]{1,0:T(8,128)(2,1)}) %all-gather.8.cloned.1.call-update) | async-done | bytes 2097168 | tf_op jit(solution)/shard_map/all_gather | solution.py:24
  254.7 7.2 convolution_bitcast_fusion
  261.9 0.0 all-reduce.7.cloned.1.call-start
  262.0 20.4 %reduce-scatter.2.cloned.1.call-done = f32[4,2048,128]{1,2,0:T(8,128)} async-done(((f32[8,2048,128]{1,2,0:T(8,128)}), f32[4,2048,128]{1,2,0:T(8,128)}) %reduce-scatter.2.cloned.1.call-update) | async-done | bytes 4194320 | tf_op jit(solution)/shard_map/reduce_scatter | solution.py:26
  282.3 2.8 select_bitcast_fusion
  285.1 0.2 all-reduce.5.cloned.1.call-start
  285.4 307.6 %all-reduce.7.cloned.1.call-done = (f32[2048,128]{0,1:T(8,128)}, f32[2048,128]{0,1:T(8,128)}) async-done(((f32[2048,128]{0,1:T(8,128)}, f32[2048,128]{0,1:T(8,128)}), (f32[2048,128]{0,1:T(8,128)}, f32[2048,128]{0,1:T(8,128)})) %all-reduce.7.cloned.1.call-update) | async-done | bytes 2097168 | tf_op jit(solution)/shard_map/psum | solution.py:11
  593.0 1.4 constant_dynamic-update-slice_fusion.1
  594.4 0.1 copy-done.1
  594.5 0.1 constant_dynamic-update-slice_fusion
  594.6 1.3 copy-done.2
  596.0 0.7 slice_select_fusion
  596.7 10.9 %copy.11 = f32[4,2048,1,128]{3,2,1,0:T(1,128)} copy(f32[4,2048,1,128]{1,3,0,2:T(8,128)} %bitcast.45) | data formatting | bytes 8388608
  607.6 74.0 %all-reduce.5.cloned.1.call-done = f32[256,256]{0,1:T(8,128)} async-done(((f32[256,256]{0,1:T(8,128)}), f32[256,256]{0,1:T(8,128)}) %all-reduce.5.cloned.1.call-update) | async-done | bytes 262160 | tf_op jit(solution)/shard_map/psum | solution.py:11
  681.6 1.1 copy.6
  682.7 1.0 fusion.2
  683.7 11.7 %cholesky.49 = f32[128,128]{1,0:T(8,128)S(1)} custom-call(f32[128,128]{1,0:T(8,128)S(1)} %cholesky.115), custom_call_target="Cholesky" | custom-call | tf_op jit(solution)/shard_map/jit(cholesky)/cholesky | solution.py:41
  695.4 9.8 %custom-call.14 = f32[1,128,128]{1,2,0:T(8,128)S(1)} custom-call(f32[1,128,128]{2,1,0:T(8,128)S(1)} %get-tuple-element.31), custom_call_target="InvertDiagBlocksLowerTriangular" | custom-call | tf_op jit(solution)/shard_map/jit(cholesky)/cholesky | solution.py:41
  705.3 0.2 fusion.7
  705.5 0.3 convolution_subtract_fusion.1
  705.7 11.7 %cholesky.103 = f32[128,128]{1,0:T(8,128)S(1)} custom-call(f32[128,128]{1,0:T(8,128)S(1)} %convolution_subtract_fusion.1), custom_call_target="Cholesky" | custom-call | tf_op jit(solution)/shard_map/jit(cholesky)/cholesky | solution.py:41
  717.5 0.1 copy.9
  717.6 0.1 copy.8
  717.7 0.1 copy.7
  717.8 0.7 compare_reduce_fusion
  719.9 0.1 triangular_solve.58
  720.0 4.3 while.1
  720.0 0.6 fusion.24
  720.6 1.4 dynamic-slice.12
  722.0 0.1 copy.16
  722.1 0.6 fusion.24
  722.8 1.4 dynamic-slice.12
  724.2 0.1 copy.16
  724.3 19.9 %custom-call.15 = f32[2,128,128]{1,2,0:T(8,128)S(1)} custom-call(f32[2,128,128]{2,1,0:T(8,128)S(1)} %get-tuple-element.9), custom_call_target="InvertDiagBlocksLowerTriangular" | custom-call | tf_op jit(solution)/shard_map/triangular_solve | solution.py:42
  744.2 1.1 fusion.6
  745.3 1.1 convolution_subtract_fusion
  746.5 0.3 fusion.4
  746.8 0.1 fusion.3
  746.8 0.7 copy.12
  (27 shorter events, 0.4 us)
Async XLA Ops:
  7.2 130.3 %copy-start = (bf16[8192,128]{1,0:T(8,128)(2,1)S(1)}, bf16[8192,128]{1,0:T(8,128)(2,1)}, u32[]{:S(2)}) copy-start(bf16[8192,128]{1,0:T(8,128)(2,1)} %param.4) | copy-start | bytes 6291460
  7.2 130.3 %all-gather.4.cloned.1.call-start = ((), (), s32[]{:S(2)}) async-start(), calls=%async_computation.1 | async-start | bytes 8912896 | tf_op jit(solution)/shard_map/all_gather | solution.py:17
  7.9 175.4 %all-gather.6.cloned.1.call-start = ((), (), s32[]{:S(2)}) async-start(), calls=%async_computation.2 | async-start | bytes 1179648 | tf_op jit(solution)/shard_map/all_gather | solution.py:25
  137.5 5.9 copy-start.3
  137.5 6.4 copy-start.4
  146.8 107.9 %all-gather.8.cloned.1.call-start = ((), (), s32[]{:S(2)}) async-start(), calls=%async_computation.3 | async-start | bytes 2228224 | tf_op jit(solution)/shard_map/all_gather | solution.py:24
  147.6 134.7 %reduce-scatter.2.cloned.1.call-start = ((), (), s32[]{:S(2)}) async-start(), calls=%async_computation.4 | async-start | bytes 12582912 | tf_op jit(solution)/shard_map/reduce_scatter | solution.py:26
  261.9 331.1 %all-reduce.7.cloned.1.call-start = ((), (), s32[]{:S(2)}) async-start(), calls=%async_computation.6 | async-start | bytes 4194304 | tf_op jit(solution)/shard_map/psum | solution.py:11
  285.1 396.5 %all-reduce.5.cloned.1.call-start = ((), (), s32[]{:S(2)}) async-start(), calls=%async_computation.5 | async-start | bytes 524288 | tf_op jit(solution)/shard_map/psum | solution.py:11
  593.0 1.5 copy-start.1
  594.6 1.3 copy-start.2
Sparse Core Ops, SparseCore 0:
  10.4 127.0 all-gather.3
  147.0 36.2 all-gather.5
  186.3 68.4 all-gather.7
  262.0 20.2 reduce-scatter.1
  285.6 307.3 all-reduce.6
  596.8 84.7 all-reduce.4
where the time goes:
time: 762 us; the launch traced here: 754 us
  waiting for transfers between devices  638 us (84%)
  other arithmetic  58.5 us (8%)
  local copies, waits for them, and re-layouts  22.3 us (3%)
  matrix products  19 us (2%)
  between operations  15.6 us (2%)
    psum x2, waiting for transfers between devices, spread(): return lax.psum(jnp.where(mine, array, jnp.zeros_like(array)), axis)  382 us
    all_gather x1, waiting for transfers between devices, local(): piece = lax.all_gather(tokens, 'col', axis=1, tiled=True)  130 us
    all_gather x1, waiting for transfers between devices, local(): row_block = lax.all_gather(hidden, 'col', axis=1, tiled=True)  69.9 us
    all_gather x1, waiting for transfers between devices, local(): lax.all_gather(hidden, 'row', axis=1, tiled=True)  35.6 us
    another operation x6, other arithmetic, local(): factor = jnp.linalg.cholesky(corner)  34 us
    reduce_scatter x1, waiting for transfers between devices, local(): lax.psum_scatter(jnp.einsum('ti,tak->aik', row_block, col_group, preferre...  20.4 us
    another operation x4, other arithmetic, local(): lax.linalg.triangular_solve(factor, own_rows, left_side=False, lower=True...  20 us
  transfers between devices with their start and end apart: 6, of which 6 were waited for; matrix products, arithmetic and copies ran while one was open for 2% of the time, Pallas kernels for 0%

commit v1 on v0

v1 whole, which is shorter than its diff:
```python
import functools

import jax
import jax.numpy as jnp
from jax import lax
from jax.experimental import pallas as pl
from jax.experimental.pallas import tpu as pltpu
from jax.sharding import PartitionSpec as P

PANEL = 256
HIGH = lax.Precision.HIGHEST
MESH = pl.DeviceIdType.MESH
OFFSETS = (0, -1, 1, 2)
NT = (((1,), (1,)), ((), ()))
F32 = jnp.float32

ROWS = 512
QUARTER = 64
FIRST_Y = (256, 96)
FIRST_Z = (352, 160)
PIECES = 4
BATCHES = (2, 2, 2, 2, 2, 2, 1, 1, 1)
RATE, HOP, ISSUE, AHEAD = 49.0, 2.0, 0.12, 0.5


class Move:
    def __init__(self, link, size, needs, source=None, target=None, rows=None, target_rows=None, role=None):
        self.link, self.size, self.needs = link, size, needs
        self.source, self.target, self.rows, self.target_rows, self.role = source, target, rows, target_rows, role


def part(rows, which):
    first = (rows[2] // 2 + 15) // 16 * 16
    return (rows[0], rows[1] + first, rows[2] - first) if which == "b" else (rows[0], rows[1], first)


def token_moves():
    moves, arrivals = {}, {}

    def add(name, link, needs0, needs1, source, target, rows, target_rows=None):
        moves[name] = Move(link, rows[2], (tuple(needs0), tuple(needs1)), source, target, rows, target_rows or rows)

    def along_z(tag, rows, j, have):
        up, far_up, down, far_down = [tag + k for k in ("u1", "u2", "d1", "d2")]
        at = {h: (h, j) for h in OFFSETS}
        add(up, "u", [up], have, (at[-1], at[0]), at[-1], rows)
        add(far_up, "u", [far_up], [up], (at[2], at[-1]), at[2], part(rows, "a"))
        add(down, "d", have, [down], (at[0], at[1]), at[1], rows)
        add(far_down, "d", [down], [far_down], (at[1], at[2]), at[2], part(rows, "b"))
        return {0: list(have), -1: [up], 1: [down], 2: [far_up, far_down]}

    def along_y(tag, rows, h, have):
        right, left, far_right, far_left = [tag + k for k in ("y+1", "y-1", "y+2", "y-2")]
        at = {j: (h, j) for j in OFFSETS}
        add(right, "y+", have, have, (at[0],) * 2, at[-1], rows)
        add(left, "y-", have, have, (at[0],) * 2, at[1], rows)
        add(far_right, "y+", [right], [right], (at[-1],) * 2, at[2], part(rows, "a"))
        add(far_left, "y-", [left], [left], (at[1],) * 2, at[2], part(rows, "b"))
        return {0: list(have), -1: [right], 1: [left], 2: [far_right, far_left]}

    for tag, rows in (("q", (0, 0, QUARTER)), ("f", (None,) + FIRST_Y)):
        near = along_y(tag, rows, 0, [])
        for j in OFFSETS:
            for h, names in along_z(tag + "%d" % j, rows, j, near[j]).items():
                arrivals[tag, h, j] = names
    near = along_z("s", (None,) + FIRST_Z, 0, [])
    for h in OFFSETS:
        for j, names in along_y("s%d" % h, (None,) + FIRST_Z, h, near[h]).items():
            arrivals["s", h, j] = names
    ready = {}
    own, before, after, across = [(d, 0, QUARTER) for d in (0, -1, 1, 2)]
    for spot in [(h, j) for h in OFFSETS for j in OFFSETS][1:]:
        have = arrivals[("q",) + spot]
        right, left, far_right, far_left = ["x%d,%d" % spot + k for k in ("x+1", "x-1", "x+2", "x-2")]
        add(right, "x+", have, have, (spot,) * 2, spot, own, before)
        add(left, "x-", have, have, (spot,) * 2, spot, own, after)
        add(far_right, "x+", [right], [right], (spot,) * 2, spot, part(before, "a"), part(across, "a"))
        add(far_left, "x-", [left], [left], (spot,) * 2, spot, part(after, "b"), part(across, "b"))
        ready[spot] = [n for kind in "qfs" for n in arrivals[(kind,) + spot]] + [right, left, far_right, far_left]
    return moves, ready


def hidden_moves():
    moves, piece, block = {}, 128 // PIECES, 128
    every = range(PIECES)

    def add(name, link, size, needs, role):
        moves[name] = Move(link, size, (tuple(needs),) * 2, role=role)

    for p in every:
        add("zl%d" % p, "zl", piece, [], ("cols", (0, "mine"), (0, "other"), "zl", p))
        for sign, d in (("+", 1), ("-", -1)):
            add("xo%s%d" % (sign, p), "x" + sign, piece, [], ("cols", (0, "mine"), (-d, "mine"), "x" + sign, p))
            add("xp%s%d" % (sign, p), "x" + sign, piece, ["zl%d" % p], ("cols", (0, "other"), (-d, "other"), "x" + sign, p))
        add("xr+%d" % p, "x+", piece, ["xo+%d" % p, "xp+%d" % p], ("cols", (-1, 0), (2, 0), "x+", p))
    add("xr-", "x-", block, ["x%s-%d" % (k, p) for k in "op" for p in every], ("cols", (1, 1), (2, 1), "x-", None))
    gone = {0: ([], []), -1: (["za+"], ["zb+"]), 1: (["za-"], ["zb-"]), 2: (["zr+"], ["zr-"])}
    for relayed, (sign, d) in enumerate((("+", 1), ("-", -1))):
        link = "u" if d == 1 else "d"
        for which, half in enumerate("ab"):
            add("z" + half + sign, link, block, [], ("rows", (0, 0), (-d, 0), "z" + sign, which))
            for h in OFFSETS:
                add("y%d" % h + half + sign, "y" + sign, block // 2, gone[h][which], ("rows", (h, 0), (h, -d), "y" + sign, which))
        add("zr" + sign, link, block, ["z" + "ab"[relayed] + sign], ("rows", (-d, 0), (2, 0), "z" + sign, relayed))
        for h in OFFSETS:
            need = ["y%d" % h + "ab"[relayed] + sign]
            add("y%dr" % h + sign, "y" + sign, block // 2, need, ("rows", (h, -d), (h, 2), "y" + sign, relayed))
    for p in every:
        first = [name % p for name in ("zl%d", "xo+%d", "xo-%d", "xp+%d", "xp-%d", "xr+%d")]
        for hop in (1, 2, 3):
            add("c%d%d" % (hop, p), "c%d" % hop, piece, first if hop == 1 else ["c%d%d" % (hop - 1, p)], ("chain", hop, p))
        add("l%d" % p, "l", piece, ["c3%d" % p], ("spread", p))
        add("m%d" % p, "m", piece, ["l%d" % p], ("relay", p))
    row_groups = {h: gone[h][0] + gone[h][1] + ["y%d" % h + k + sign for k in "abr" for sign in "+-"] for h in OFFSETS}
    pairs = {0: ["zl%d" % p for p in every], 2: ["xr-"] + ["xr+%d" % p for p in every]}
    for sign, d in (("+", -1), ("-", 1)):
        pairs[d] = ["x%s%s%d" % (k, sign, p) for k in "op" for p in every]
    return moves, row_groups, pairs


def schedule(moves):
    followers = {name: set() for name in moves}
    for name, move in moves.items():
        for parity in (0, 1):
            for need in move.needs[parity]:
                followers[need].add((name, parity))

    def there(name, parity):
        return 1 - parity if moves[name].role is None and moves[name].link in "ud" else parity

    @functools.lru_cache(None)
    def rest(name, parity):
        after = [moves[m].size / RATE + HOP + rest(m, there(m, q)) for m, q in followers[name] if q == parity]
        return max(after, default=0.0)

    landed, begun, free = ({}, {}), ({}, {}), {}
    waiting = {(name, parity) for name in moves for parity in (0, 1)}
    while waiting:
        best = None
        for name, parity in waiting:
            move, have = moves[name], landed[parity]
            when = max(free.get((move.link, parity), 0.0), free.get(parity, 0.0))
            for need in move.needs[parity]:
                if need not in have:
                    break
                when = max(when, have[need])
            else:
                key = (when, -(rest(name, there(name, parity)) + move.size / RATE), name, parity)
                if best is None or key < best:
                    best = key
        when, _, name, parity = best
        done = when + moves[name].size / RATE
        free[moves[name].link, parity] = done
        free[parity] = when + ISSUE
        begun[parity][name] = when
        landed[there(name, parity)][name] = done + HOP
        waiting.discard((name, parity))
    return begun, landed


def eliminate(u, piece):
    wide = lax.broadcasted_iota(jnp.int32, (8, 384), 0)
    base = 64 * (piece // 2)
    groups = [u[base + 8 * g:base + 8 * g + 8, :] for g in range(8)]
    for p in range(4 * (piece % 2), 4 * (piece % 2) + 4):
        cols = {
            (g, k): jnp.broadcast_to(groups[g][:, base + 8 * p + k:base + 8 * p + k + 1], (8, 128))
            for g in range(p, 8) for k in range(8)
        }
        for k in range(8):
            inv = lax.rsqrt(jnp.broadcast_to(cols[p, k][k:k + 1, :], (8, 128)))
            inv2 = inv * inv
            ratio = [cols[g, k] * inv2 for g in range(p, 8)]
            for j in range(k + 1, 8):
                pivot = jnp.broadcast_to(cols[p, k][j:j + 1, :], (8, 128))
                for g in range(p, 8):
                    cols[g, j] = cols[g, j] - ratio[g - p] * pivot
            line = jnp.broadcast_to(groups[p][k:k + 1, :], (8, 384))
            scaled = groups[p] * jnp.concatenate([inv] * 3, axis=1)
            lower = jnp.concatenate([ratio[0]] * 3, axis=1)
            groups[p] = jnp.where(wide == k, scaled, jnp.where(wide > k, groups[p] - lower * line, groups[p]))
            for g in range(p, 8):
                cols[g, k] = cols[g, k] * inv
        for g in range(p + 1, 8):
            acc = groups[g]
            for k in range(8):
                acc = acc - jnp.concatenate([cols[g, k]] * 3, axis=1) * jnp.broadcast_to(groups[p][k:k + 1, :], (8, 384))
            groups[g] = acc
    for g in range(4 * (piece % 2), 8):
        u[base + 8 * g:base + 8 * g + 8, :] = groups[g]
    if piece % 2 and piece < 7:
        block = u[base:base + 64, :]
        first = 0 if base == 0 else 128
        update = jnp.dot(block[:, first:256].T, block, precision=HIGH, preferred_element_type=F32)
        rest = base + 64
        u[rest:256, :] = u[rest:256, :] - update[rest - first:256 - first, :]


def gather_kernel(
    tokens_hbm, gate_hbm, up_hbm, rows_out, cols_out, lead_out, own_out,
    held, weights, total, rows, cols, leads,
    load_sem, send_sem, recv_sem, send2, recv2, side_send, side_recv, lead_send, lead_recv, local_sem,
):
    tok, row, col = lax.axis_index("tok"), lax.axis_index("row"), lax.axis_index("col")
    x, z_lo, z_hi, y = lax.div(row, 2), lax.rem(row, 2), lax.div(col, 4), lax.rem(col, 4)

    def around(at):
        return {0: at, 1: lax.rem(at + 1, 4), 2: lax.rem(at + 2, 4), -1: lax.rem(at + 3, 4)}

    xs, zs, ys = around(x), around(z_hi), around(y)
    places = {(h, j): zs[h] * 4 + ys[j] for h in OFFSETS for j in OFFSETS}
    quarters = {d: xs[d] * QUARTER for d in OFFSETS}
    groups = {(d, z): xs[d] * 2 + z for d in OFFSETS for z in (0, 1)}
    firsts = {h: zs[h] * 4 for h in OFFSETS}
    spots = {d: lax.rem(xs[d], 2) * 2 for d in OFFSETS}
    keeps = {d: lax.div(xs[d], 2) == tok for d in OFFSETS}
    partner_row = x * 2 + 1 - z_lo

    devices = {"zl": (tok, partner_row, col)}
    for sign, d in (("+", 1), ("-", -1)):
        devices["x" + sign] = (tok, xs[d] * 2 + z_lo, col)
        devices["y" + sign] = (tok, row, places[0, d])
        devices["z" + sign] = (tok, row, places[d, 0])
    sibling = (1 - tok, row, col)
    step = {
        ("u", 0): devices["zl"], ("u", 1): (tok, partner_row, places[1, 0]),
        ("d", 0): (tok, partner_row, places[-1, 0]), ("d", 1): devices["zl"],
    }
    low = y < 2
    at_z = {k: jnp.logical_and(low, z_hi == k) for k in range(4)}
    past_first = jnp.logical_and(low, z_hi > 0)
    at_y = {k: y == k for k in range(4)}

    first = pltpu.make_async_copy(tokens_hbm, held.at[col], load_sem.at[2])
    first.start()
    loads = [
        pltpu.make_async_copy(gate_hbm, weights.at[:, 0:128], load_sem.at[0]),
        pltpu.make_async_copy(up_hbm, weights.at[:, 128:256], load_sem.at[1]),
    ]
    for load in loads:
        load.start()

    barrier = pltpu.get_barrier_semaphore()
    far = (tok, partner_row, places[1, 0] * z_lo + places[-1, 0] * (1 - z_lo))
    near = [devices[k] for k in ("x+", "x-", "y+", "y-", "z+", "z-", "zl")] + [far, sibling]
    for device in near:
        pl.semaphore_signal(barrier, inc=1, device_id=device, device_id_type=MESH)
    pl.semaphore_wait(barrier, len(near))
    first.wait()

    tokens, ready = token_moves()
    hiddens, row_groups, pairs = hidden_moves()
    number = {name: at for at, name in enumerate(tokens)}
    number.update({name: at for at, name in enumerate(n for n in hiddens if hiddens[n].role[0] in ("rows", "cols"))})

    def span(at_rows):
        if at_rows[0] is None:
            return pl.ds(at_rows[1], at_rows[2])
        return pl.ds(pl.multiple_of(quarters[at_rows[0]] + at_rows[1], 16), at_rows[2])

    def remote(semaphores, index, source, target, device):
        return pltpu.make_async_remote_copy(
            src_ref=source, dst_ref=target, send_sem=semaphores[0].at[index], recv_sem=semaphores[1].at[index],
            device_id=device, device_id_type=MESH,
        )

    def held_ref(spot, at_rows):
        return held.at[places[spot], span(at_rows), :]

    def block_ref(move, at, parity):
        kind, which = move.role[0], move.role[4]
        if kind == "rows":
            return rows.at[places[at]] if which is None else rows.at[places[at], pl.ds(64 * which, 64), :]
        z = {"mine": parity, "other": 1 - parity}.get(at[1], at[1])
        if which is None:
            return cols.at[groups[at[0], z]]
        size = 128 // PIECES
        return cols.at[groups[at[0], z], pl.ds(size * which, size), :]

    def outgoing(move, name, parity):
        if move.role is not None:
            place = block_ref(move, move.role[1], parity)
            return remote((send2, recv2), number[name], place, place, devices[move.role[3]])
        place = held_ref(move.source[parity], move.rows)
        device = step[move.link, parity] if move.link in "ud" else devices[move.link]
        return remote((send_sem, recv_sem), number[name], place, place, device)

    def incoming(move, name, parity):
        if move.role is not None:
            place = block_ref(move, move.role[2], parity)
            return remote((send2, recv2), number[name], place, place, sibling)
        place = held_ref(move.target, move.target_rows)
        return remote((send_sem, recv_sem), number[name], place, place, sibling)

    def lead(b, p):
        size = 128 // PIECES
        return leads.at[b, pl.ds(size * p, size), :]

    def lead_copy(kind, b, p, device, from_cols=False):
        size = 128 // PIECES
        return pltpu.make_async_remote_copy(
            src_ref=cols.at[0, pl.ds(size * p, size), :] if from_cols else lead(b, p), dst_ref=lead(b, p),
            send_sem=lead_send.at[kind * PIECES + p],
            recv_sem=lead_recv.at[b * PIECES + p],
            device_id=device, device_id_type=MESH,
        )

    def lead_arrive(b, p):
        lead_copy(0, b, p, sibling).wait_recv()

    def chain_role(hop, parity):
        if hop == 1:
            return at_z[0], step["u" if parity == 1 else "d", parity]
        upward = (hop == 2) == (parity == 0)
        return at_z[1 if upward else 3], step["u" if upward else "d", parity]

    relays = ((3, 0, "y-"), (2, 1, "y+"))

    def lead_start(role, parity):
        if role[0] == "chain":
            hop, p = role[1:]
            here, device = chain_role(hop, parity)

            @pl.when(here)
            def _():
                if hop > 1:
                    lead_arrive(y, p)
                lead_copy(0, y, p, device, hop == 1).start()
        elif role[0] == "spread":
            p = role[1]

            @pl.when(at_z[0])
            def _():
                lead_copy(1, y, p, devices["y+"], True).start()
                lead_copy(2, y, p, devices["y-"], True).start()

            @pl.when(at_z[2])
            def _():
                lead_arrive(y, p)

            @pl.when(past_first)
            def _():
                lead_copy(1, y, p, devices["y+"]).start()
                lead_copy(2, y, p, devices["y-"]).start()
        else:
            p = role[1]
            for k, b, way in relays:
                @pl.when(at_y[k])
                def _():
                    lead_arrive(b, p)
                    lead_copy(3, b, p, devices[way]).start()

    def lead_end(parity):
        for p in range(PIECES):
            for hop in (1, 2, 3):
                here, device = chain_role(hop, parity)

                @pl.when(here)
                def _():
                    lead_copy(0, y, p, device).wait_send()

            @pl.when(low)
            def _():
                lead_copy(1, y, p, devices["y+"]).wait_send()
                lead_copy(2, y, p, devices["y-"]).wait_send()

            for k, b, way in relays:
                @pl.when(at_y[k])
                def _():
                    lead_copy(3, b, p, devices[way]).wait_send()

    def side(index, source, target):
        return pltpu.make_async_remote_copy(
            src_ref=source, dst_ref=target, send_sem=side_send.at[index], recv_sem=side_recv.at[index],
            device_id=sibling, device_id_type=MESH,
        )

    def keep(index, source, target):
        return pltpu.make_async_copy(source, target, local_sem.at[index])

    shared = {}
    for k, h in enumerate(OFFSETS):
        shared["r", h] = (row_groups[h], k)
        shared["c", h] = (pairs[h], 4 + k)

    def side_refs(kind, d):
        if kind == "r":
            at = pl.ds(firsts[d], 4)
            return rows.at[at], (lambda t: rows_out.at[t, at])
        if kind == "c":
            return cols.at[pl.ds(groups[d, 0], 2)], (lambda t: cols_out.at[t, pl.ds(spots[d], 2)])
        if kind == "l":
            return leads, (lambda t: lead_out.at[t])
        return rows.at[col], (lambda t: own_out.at[t])

    def side_start(kind, d, index):
        source, target = side_refs(kind, d)
        if kind != "c":
            side(index, source, target(tok)).start()
            keep(index, source, target(tok)).start()
            return

        @pl.when(keeps[d])
        def _():
            keep(index, source, target(tok)).start()

        @pl.when(jnp.logical_not(keeps[d]))
        def _():
            side(index, source, target(tok)).start()

    def side_end(kind, d, index):
        source, target = side_refs(kind, d)
        if kind != "c":
            side(index, target(1 - tok), target(1 - tok)).wait_recv()
            side(index, source, target(tok)).wait_send()
            keep(index, source, target(tok)).wait()
            return

        @pl.when(keeps[d])
        def _():
            keep(index, source, target(tok)).wait()
            side(index, target(1 - tok), target(1 - tok)).wait_recv()

        @pl.when(jnp.logical_not(keeps[d]))
        def _():
            side(index, source, target(tok)).wait_send()

    def both(act):
        for parity in (0, 1):
            pl.when(z_lo == parity)(functools.partial(act, parity))

    def in_order(begun):
        return [sorted((begun[parity][name], name) for name in begun[parity]) for parity in (0, 1)]

    begun, landed = schedule(tokens)
    order = in_order(begun)
    seen, at = (set(), set()), [0, 0]

    def arrive(moves, name, parity):
        if name not in seen[parity]:
            seen[parity].add(name)
            if name in number:
                incoming(moves[name], name, parity).wait_recv()

    def stretch(until, batch, parity):
        while at[parity] < len(order[parity]) and order[parity][at[parity]][0] <= until:
            name = order[parity][at[parity]][1]
            at[parity] += 1
            for need in tokens[name].needs[parity]:
                arrive(tokens, need, parity)
            outgoing(tokens[name], name, parity).start()
        for chunk in batch:
            for need in ready[chunk]:
                arrive(tokens, need, parity)

    finished = {c: max(landed[p][name] for p in (0, 1) for name in ready[c]) for c in ready}
    queue = sorted(ready, key=lambda c: (finished[c], c))
    start = 0
    for k, size in enumerate(BATCHES):
        batch = queue[start:start + size]
        start += size
        until = max(finished[c] for c in batch) + AHEAD if start < len(queue) else 1e9
        both(functools.partial(stretch, until, batch))
        if k == 0:
            for load in loads:
                load.wait()
            total[...] = jnp.zeros_like(total)
        for here in ([col] if k == 0 else []) + [places[chunk] for chunk in batch]:
            total[...] += jnp.dot(held[here], weights[pl.ds(pl.multiple_of(here * 512, 512), 512), :], preferred_element_type=F32)

    def tokens_end(parity):
        for name in tokens:
            arrive(tokens, name, parity)

    both(tokens_end)
    gate = total[:, 0:128]
    hidden = gate / (1.0 + jnp.exp(-gate)) * total[:, 128:256]
    hidden = hidden.T.astype(jnp.bfloat16)
    rows[col] = hidden
    cols[row] = hidden

    begun, landed = schedule(hiddens)
    order = in_order(begun)
    left = (dict(shared), dict(shared))

    def hidden_stage(parity):
        waited = False
        for _, name in order[parity]:
            move = hiddens[name]
            if move.needs[parity] and not waited:
                waited = True
                side_start("o", 0, 8)
                for sent in tokens:
                    outgoing(tokens[sent], sent, parity).wait_send()
            for need in move.needs[parity]:
                arrive(hiddens, need, parity)
            if move.role[0] in ("rows", "cols"):
                outgoing(move, name, parity).start()
            else:
                lead_start(move.role, parity)
            for key in list(left[parity]):
                names, index = left[parity][key]
                if seen[parity].issuperset(names):
                    del left[parity][key]
                    side_start(*key, index)
        for key in list(left[parity]):
            names, index = left[parity].pop(key)
            for name in names:
                arrive(hiddens, name, parity)
            side_start(*key, index)
        for name in hiddens:
            arrive(hiddens, name, parity)

    both(hidden_stage)
    held_lead = pltpu.make_async_copy(cols.at[0], leads.at[lax.rem(y, 2)], local_sem.at[10])

    @pl.when(at_z[0])
    def _():
        held_lead.start()

    for p in range(PIECES):
        for k, b in ((0, 1), (1, 0), (2, 0), (3, 1)):
            @pl.when(at_y[k])
            def _():
                lead_arrive(b, p)

    @pl.when(at_z[0])
    def _():
        held_lead.wait()

    side_start("l", 0, 9)

    def hidden_end(parity):
        lead_end(parity)
        for name in hiddens:
            if name in number:
                outgoing(hiddens[name], name, parity).wait_send()

    both(hidden_end)
    for kind, d in shared:
        side_end(kind, d, shared[kind, d][1])
    side_end("o", 0, 8)
    side_end("l", 0, 9)


def gather(tokens, gate_weight, up_weight):
    depth, width = gate_weight.shape
    half = tokens.shape[0]
    bf16 = jnp.bfloat16
    hbm = pl.BlockSpec(memory_space=pl.ANY)
    return pl.pallas_call(
        gather_kernel,
        out_shape=(
            jax.ShapeDtypeStruct((2, 16, width, half), bf16),
            jax.ShapeDtypeStruct((2, 4, width, half), bf16),
            jax.ShapeDtypeStruct((2, 2, width, half), bf16),
            jax.ShapeDtypeStruct((2, width, half), bf16),
        ),
        in_specs=[hbm, hbm, hbm],
        out_specs=(hbm,) * 4,
        scratch_shapes=[
            pltpu.VMEM((16, half, 512), bf16),
            pltpu.VMEM((depth, 2 * width), bf16),
            pltpu.VMEM((half, 2 * width), F32),
            pltpu.VMEM((16, width, half), bf16),
            pltpu.VMEM((8, width, half), bf16),
            pltpu.VMEM((2, width, half), bf16),
            pltpu.SemaphoreType.DMA((3,)),
            pltpu.SemaphoreType.DMA((120,)),
            pltpu.SemaphoreType.DMA((120,)),
            pltpu.SemaphoreType.DMA((55,)),
            pltpu.SemaphoreType.DMA((55,)),
            pltpu.SemaphoreType.DMA((10,)),
            pltpu.SemaphoreType.DMA((10,)),
            pltpu.SemaphoreType.DMA((4 * PIECES,)),
            pltpu.SemaphoreType.DMA((2 * PIECES,)),
            pltpu.SemaphoreType.DMA((11,)),
        ],
        compiler_params=pltpu.CompilerParams(
            collective_id=0, has_side_effects=True, vmem_limit_bytes=60 * 2**20
        ),
        cost_estimate=pl.CostEstimate(flops=2 * half * depth * 2 * width, bytes_accessed=12 * 2**20, transcendentals=half * width),
    )(tokens, gate_weight, up_weight)


def gram_kernel(rows_ref, cols_ref, lead_ref, own_ref, gram_ref, panel_ref, u, out):
    step = pl.program_id(0)

    def tile():
        both = rows_ref[...].reshape(2, 256, 512)
        right = cols_ref[...].reshape(2, 512, 512)
        product = lax.dot_general(both[0], right[0], NT, preferred_element_type=F32)
        product += lax.dot_general(both[1], right[1], NT, preferred_element_type=F32)
        for a in range(4):
            gram_ref[a] = product[:, 128 * a:128 * a + 128]

    @pl.when(step == 0)
    def _():
        lead = lead_ref[...].reshape(2, 256, 512)
        u[:, 0:256] = lax.dot_general(lead[0], lead[0], NT, preferred_element_type=F32) + lax.dot_general(lead[1], lead[1], NT, preferred_element_type=F32)
        u[:, 256:384] = lax.dot_general(lead[0], own_ref[0], NT, preferred_element_type=F32) + lax.dot_general(lead[1], own_ref[1], NT, preferred_element_type=F32)

    for part_at in range(8):
        @pl.when(step == part_at)
        def _():
            tile()
            eliminate(u, part_at)

    @pl.when(step == 7)
    def _():
        panel_ref[...] = u[pl.ds(pl.multiple_of(lax.axis_index("tok") * 128, 128), 128), 256:384].T


def gram_and_panel(rows, cols, lead, own):
    width, half = rows.shape[2:]
    return pl.pallas_call(
        gram_kernel,
        grid=(8,),
        out_shape=(
            jax.ShapeDtypeStruct((4, 16 * width, width), F32),
            jax.ShapeDtypeStruct((width, width), F32),
        ),
        in_specs=[
            pl.BlockSpec((2, 2, width, half), lambda s: (0, s, 0, 0)),
            pl.BlockSpec((2, 4, width, half), lambda s: (0, 0, 0, 0)),
            pl.BlockSpec((2, 2, width, half), lambda s: (0, 0, 0, 0)),
            pl.BlockSpec((2, width, half), lambda s: (0, 0, 0)),
        ],
        out_specs=(
            pl.BlockSpec((4, 2 * width, width), lambda s: (0, s, 0)),
            pl.BlockSpec((width, width), lambda s: (0, 0)),
        ),
        scratch_shapes=[pltpu.VMEM((PANEL, 384), F32), pltpu.VMEM((8, 128), F32)],
        compiler_params=pltpu.CompilerParams(vmem_limit_bytes=60 * 2**20),
        cost_estimate=pl.CostEstimate(flops=2 * 2048 * 512 * 1024, bytes_accessed=10 * 2**20, transcendentals=0),
    )(rows, cols, lead, own)


def local(tokens, gate_weight, up_weight):
    gram, panel = gram_and_panel(*gather(tokens, gate_weight, up_weight))
    return (gram.reshape(4, 2048, 1, 128), panel)


def solution(mesh):
    placed = (P("tok", "col"), P(None, ("row", "col")), P(None, ("row", "col")))
    return jax.shard_map(
        local,
        mesh=mesh,
        in_specs=placed,
        out_specs=(P("tok", "row", "col", None), P(("row", "col"), "tok")),
        check_vma=False,
    )
```

time: 762 us -> 92.9 us (0.12)
  waiting for transfers between devices: 638 us -> 0 us
  Pallas kernels: 0 us -> 92.1 us
  other arithmetic: 58.5 us -> 0 us
  local copies, waits for them, and re-layouts: 22.3 us -> 0 us
  matrix products: 19 us -> 0 us
  between operations: 15.6 us -> 0.64 us
    psum x2 -> x0, waiting for transfers between devices: 382 us -> none  [spread(): return lax.psum(jnp.where(mine, array, jnp.zeros_like(array)), axis)]
    all_gather x3 -> x0, waiting for transfers between devices: 235 us -> none  [the longest x1 130 us: local(): piece = lax.all_gather(tokens, 'col', axis=1, tiled=True)]
    pallas_call x0 -> x2, Pallas kernels: none -> 92.1 us  [the longest x1 79.6 us: gather(): pl.pallas_call(gather_kernel, out_shape=(jax.ShapeDtypeStruct((2, 16, wid...]
    another operation x10 -> x0, other arithmetic: 54 us -> none  [the longest x6 34 us: local(): factor = jnp.linalg.cholesky(corner)]
    reduce_scatter x1 -> x0, waiting for transfers between devices: 20.4 us -> none  [local(): lax.psum_scatter(jnp.einsum('ti,tak->aik', row_block, col_group, preferre...]
    dot_general x3 -> x0, matrix products: 16 us -> none  [the longest x1 7.16 us: local(): jnp.einsum('ti,tak->aik', row_block, col_group, preferred_element_type=jn...]
    unnamed x13 -> x0, local copies, waits for them, and re-layouts: 15 us -> none
  transfers between devices with their start and end apart: 6 -> 0, of which waited for: 6 -> 0; matrix products, arithmetic and copies ran while one was open for 2% -> 0% of each run, Pallas kernels for 0% -> 0%
where the time goes in v1:
time: 92.9 us; the launch traced here: 92.7 us
  Pallas kernels  92.1 us (99%)
    pallas_call x1, Pallas kernels, gather(): pl.pallas_call(gather_kernel, out_shape=(jax.ShapeDtypeStruct((2, 16, wid...  79.6 us
    pallas_call x1, Pallas kernels, gram_and_panel(): pl.pallas_call(gram_kernel, grid=(8,), out_shape=(jax.ShapeDtypeStruct((4...  12.5 us

profile of v1, /device:TPU:27, one launch (start us, length us, event | category | flops | bytes accessed | tf_op | source)
XLA Modules:
  0.0 92.7 jit_solution(2400637511007077975)
XLA Ops:
  0.6 79.6 %shard_map.50 = (bf16[2,16,128,512]{3,2,1,0:T(8,128)(2,1)}, bf16[2,4,128,512]{3,2,1,0:T(8,128)(2,1)}, bf16[2,2,128,512]{3,2,1,0:T(8,128)(2,1)}, bf16[2,128,512]{2,1,0:T(8,128)(2,1)}) custom-call(bf16[512,512]{1,0:T(8,128)(2,1)} %tokens_hbm.1, bf16[8192,128]{1,0:T(8,128)(2,1)} %gate_hbm.1, bf16[8192,128]{1,0:T(8,128)(2,1)} %up_hbm.1), custom_call_target="tpu_custom_call" | custom-call | flops 2147483648 | bytes 12582912 | tf_op jit(solution)/shard_map/pallas_call | solution.py:551
  80.3 12.5 %shard_map.51 = (f32[4,2048,128]{2,1,0:T(8,128)}, f32[128,128]{1,0:T(8,128)}) custom-call(bf16[2,16,128,512]{3,2,1,0:T(8,128)(2,1)} %get-tuple-element.8.rows_ref, bf16[2,4,128,512]{3,2,1,0:T(8,128)(2,1)} %get-tuple-element.9.cols_ref, bf16[2,2,128,512]{3,2,1,0:T(8,128)(2,1)} %get-tuple-element.10.lead_ref, bf16[2,128,512]{2,1,0:T(8,128)(2,1)} %get-tuple-element.11.own_ref), custom_call_target="tpu_custom_call" | custom-call | flops 2147483648 | bytes 10485760 | tf_op jit(solution)/shard_map/pallas_call | solution.py:616

commit v2 on v1

--- a/solution.py
+++ b/solution.py
@@ -158,33 +158,58 @@
     return begun, landed
 
 
+def balance(u):
+    rows = lax.broadcasted_iota(jnp.int32, (PANEL, PANEL), 0)
+    lanes = lax.broadcasted_iota(jnp.int32, (PANEL, PANEL), 1)
+    corner = u[:, 0:PANEL]
+    only = jnp.where(rows == lanes, corner, 0.0)
+    down, across = lax.rsqrt(jnp.sum(only, axis=1, keepdims=True)), lax.rsqrt(jnp.sum(only, axis=0, keepdims=True))
+    u[:, 0:PANEL] = corner * down * across
+    u[:, PANEL:] = u[:, PANEL:] * down
+
+
 def eliminate(u, piece):
     wide = lax.broadcasted_iota(jnp.int32, (8, 384), 0)
     base = 64 * (piece // 2)
     groups = [u[base + 8 * g:base + 8 * g + 8, :] for g in range(8)]
+
+    def spread(row, at):
+        return jnp.broadcast_to(row[at:at + 1, :], (8, row.shape[1]))
+
+    def thrice(tile):
+        return jnp.concatenate([tile] * 3, axis=1)
+
     for p in range(4 * (piece % 2), 4 * (piece % 2) + 4):
         cols = {
             (g, k): jnp.broadcast_to(groups[g][:, base + 8 * p + k:base + 8 * p + k + 1], (8, 128))
             for g in range(p, 8) for k in range(8)
         }
-        for k in range(8):
-            inv = lax.rsqrt(jnp.broadcast_to(cols[p, k][k:k + 1, :], (8, 128)))
-            inv2 = inv * inv
-            ratio = [cols[g, k] * inv2 for g in range(p, 8)]
-            for j in range(k + 1, 8):
-                pivot = jnp.broadcast_to(cols[p, k][j:j + 1, :], (8, 128))
+        for k in range(0, 8, 2):
+            a, b, c = spread(cols[p, k], k), spread(cols[p, k + 1], k), spread(cols[p, k + 1], k + 1)
+            over = 1.0 / (a * c - b * b)
+            left, right = [], []
+            for g in range(p, 8):
+                left.append((c * cols[g, k] - b * cols[g, k + 1]) * over)
+                right.append((a * cols[g, k + 1] - b * cols[g, k]) * over)
+            for j in range(k + 2, 8):
+                one, two = spread(cols[p, k], j), spread(cols[p, k + 1], j)
                 for g in range(p, 8):
-                    cols[g, j] = cols[g, j] - ratio[g - p] * pivot
-            line = jnp.broadcast_to(groups[p][k:k + 1, :], (8, 384))
-            scaled = groups[p] * jnp.concatenate([inv] * 3, axis=1)
-            lower = jnp.concatenate([ratio[0]] * 3, axis=1)
-            groups[p] = jnp.where(wide == k, scaled, jnp.where(wide > k, groups[p] - lower * line, groups[p]))
+                    cols[g, j] = cols[g, j] - (left[g - p] * one + right[g - p] * two)
+            first = lax.rsqrt(a)
+            ratio = b * first * first
+            second = lax.rsqrt(c - b * ratio)
+            line, below = spread(groups[p], k), spread(groups[p], k + 1)
+            top = line * thrice(first)
+            low = (below - thrice(ratio) * line) * thrice(second)
+            rest = groups[p] - (thrice(left[0]) * line + thrice(right[0]) * below)
+            groups[p] = jnp.where(wide == k, top, jnp.where(wide == k + 1, low, jnp.where(wide > k + 1, rest, groups[p])))
             for g in range(p, 8):
-                cols[g, k] = cols[g, k] * inv
+                cols[g, k + 1] = (cols[g, k + 1] - ratio * cols[g, k]) * second
+                cols[g, k] = cols[g, k] * first
         for g in range(p + 1, 8):
             acc = groups[g]
             for k in range(8):
-                acc = acc - jnp.concatenate([cols[g, k]] * 3, axis=1) * jnp.broadcast_to(groups[p][k:k + 1, :], (8, 384))
+                acc = acc - thrice(cols[g, k]) * spread(groups[p], k)
             groups[g] = acc
     for g in range(4 * (piece % 2), 8):
         u[base + 8 * g:base + 8 * g + 8, :] = groups[g]
@@ -599,6 +624,7 @@
         lead = lead_ref[...].reshape(2, 256, 512)
         u[:, 0:256] = lax.dot_general(lead[0], lead[0], NT, preferred_element_type=F32) + lax.dot_general(lead[1], lead[1], NT, preferred_element_type=F32)
         u[:, 256:384] = lax.dot_general(lead[0], own_ref[0], NT, preferred_element_type=F32) + lax.dot_general(lead[1], own_ref[1], NT, preferred_element_type=F32)
+        balance(u)
 
     for part_at in range(8):
         @pl.when(step == part_at)

time: 92.9 us -> 93 us (level)
  no operation moved by 1% of the time
where the time goes in v2:
time: 93 us; the launch traced here: 92.8 us
  Pallas kernels  92.1 us (99%)
    pallas_call x1, Pallas kernels, gather(): pl.pallas_call(gather_kernel, out_shape=(jax.ShapeDtypeStruct((2, 16, wid...  79.6 us
    pallas_call x1, Pallas kernels, gram_and_panel(): pl.pallas_call(gram_kernel, grid=(8,), out_shape=(jax.ShapeDtypeStruct((4...  12.5 us

profile of v2, /device:TPU:27, one launch (start us, length us, event | category | flops | bytes accessed | tf_op | source)
XLA Modules:
  0.0 92.8 jit_solution(3309579705935906541)
XLA Ops:
  0.6 79.6 %shard_map.50 = (bf16[2,16,128,512]{3,2,1,0:T(8,128)(2,1)}, bf16[2,4,128,512]{3,2,1,0:T(8,128)(2,1)}, bf16[2,2,128,512]{3,2,1,0:T(8,128)(2,1)}, bf16[2,128,512]{2,1,0:T(8,128)(2,1)}) custom-call(bf16[512,512]{1,0:T(8,128)(2,1)} %tokens_hbm.1, bf16[8192,128]{1,0:T(8,128)(2,1)} %gate_hbm.1, bf16[8192,128]{1,0:T(8,128)(2,1)} %up_hbm.1), custom_call_target="tpu_custom_call" | custom-call | flops 2147483648 | bytes 12582912 | tf_op jit(solution)/shard_map/pallas_call | solution.py:576
  80.3 12.5 %shard_map.51 = (f32[4,2048,128]{2,1,0:T(8,128)}, f32[128,128]{1,0:T(8,128)}) custom-call(bf16[2,16,128,512]{3,2,1,0:T(8,128)(2,1)} %get-tuple-element.8.rows_ref, bf16[2,4,128,512]{3,2,1,0:T(8,128)(2,1)} %get-tuple-element.9.cols_ref, bf16[2,2,128,512]{3,2,1,0:T(8,128)(2,1)} %get-tuple-element.10.lead_ref, bf16[2,128,512]{2,1,0:T(8,128)(2,1)} %get-tuple-element.11.own_ref), custom_call_target="tpu_custom_call" | custom-call | flops 2147483648 | bytes 10485760 | tf_op jit(solution)/shard_map/pallas_call | solution.py:642

commit v3 on v2

--- a/solution.py
+++ b/solution.py
@@ -206,10 +206,11 @@
             for g in range(p, 8):
                 cols[g, k + 1] = (cols[g, k + 1] - ratio * cols[g, k]) * second
                 cols[g, k] = cols[g, k] * first
+        lines = [spread(groups[p], k) for k in range(8)]
         for g in range(p + 1, 8):
             acc = groups[g]
             for k in range(8):
-                acc = acc - thrice(cols[g, k]) * spread(groups[p], k)
+                acc = acc - thrice(cols[g, k]) * lines[k]
             groups[g] = acc
     for g in range(4 * (piece % 2), 8):
         u[base + 8 * g:base + 8 * g + 8, :] = groups[g]
@@ -285,7 +286,7 @@
 
     def remote(semaphores, index, source, target, device):
         return pltpu.make_async_remote_copy(
-            src_ref=source, dst_ref=target, send_sem=semaphores[0].at[index], recv_sem=semaphores[1].at[index],
+            src_ref=source, dst_ref=target, send_sem=semaphores[0].at[0], recv_sem=semaphores[1].at[index],
             device_id=device, device_id_type=MESH,
         )
 
@@ -515,8 +516,6 @@
             if move.needs[parity] and not waited:
                 waited = True
                 side_start("o", 0, 8)
-                for sent in tokens:
-                    outgoing(tokens[sent], sent, parity).wait_send()
             for need in move.needs[parity]:
                 arrive(hiddens, need, parity)
             if move.role[0] in ("rows", "cols"):
@@ -555,13 +554,10 @@
 
     side_start("l", 0, 9)
 
-    def hidden_end(parity):
-        lead_end(parity)
-        for name in hiddens:
-            if name in number:
-                outgoing(hiddens[name], name, parity).wait_send()
-
-    both(hidden_end)
+    remote((send_sem, recv_sem), 0, held.at[pl.ds(0, 15)], held.at[pl.ds(0, 15)], sibling).wait_send()
+    gone = weights.at[pl.ds(0, 5632), :]
+    remote((send2, recv2), 0, gone, gone, sibling).wait_send()
+    both(lead_end)
     for kind, d in shared:
         side_end(kind, d, shared[kind, d][1])
     side_end("o", 0, 8)
@@ -591,9 +587,9 @@
             pltpu.VMEM((8, width, half), bf16),
             pltpu.VMEM((2, width, half), bf16),
             pltpu.SemaphoreType.DMA((3,)),
+            pltpu.SemaphoreType.DMA((1,)),
             pltpu.SemaphoreType.DMA((120,)),
-            pltpu.SemaphoreType.DMA((120,)),
-            pltpu.SemaphoreType.DMA((55,)),
+            pltpu.SemaphoreType.DMA((1,)),
             pltpu.SemaphoreType.DMA((55,)),
             pltpu.SemaphoreType.DMA((10,)),
             pltpu.SemaphoreType.DMA((10,)),
@@ -608,29 +604,44 @@
     )(tokens, gate_weight, up_weight)
 
 
-def gram_kernel(rows_ref, cols_ref, lead_ref, own_ref, gram_ref, panel_ref, u, out):
+def gram_kernel(rows_hbm, cols_hbm, lead_ref, own_ref, gram_ref, panel_ref, u, rows, cols, sems):
     step = pl.program_id(0)
 
-    def tile():
-        both = rows_ref[...].reshape(2, 256, 512)
-        right = cols_ref[...].reshape(2, 512, 512)
-        product = lax.dot_general(both[0], right[0], NT, preferred_element_type=F32)
-        product += lax.dot_general(both[1], right[1], NT, preferred_element_type=F32)
+    def fetch(k):
+        if k == 8:
+            return pltpu.make_async_copy(cols_hbm, cols, sems.at[8])
+        pair = pl.ds(2 * k, 2)
+        return pltpu.make_async_copy(rows_hbm.at[:, pair], rows.at[:, pair], sems.at[k])
+
+    def product(left, right):
+        return sum(lax.dot_general(left(t), right(t), NT, preferred_element_type=F32) for t in (0, 1))
+
+    def tile(k):
+        fetch(k).wait()
+        whole = product(lambda t: rows[t, 2 * k:2 * k + 2].reshape(256, 512), lambda t: cols[t].reshape(512, 512))
         for a in range(4):
-            gram_ref[a] = product[:, 128 * a:128 * a + 128]
+            gram_ref[a] = whole[:, 128 * a:128 * a + 128]
 
     @pl.when(step == 0)
     def _():
-        lead = lead_ref[...].reshape(2, 256, 512)
-        u[:, 0:256] = lax.dot_general(lead[0], lead[0], NT, preferred_element_type=F32) + lax.dot_general(lead[1], lead[1], NT, preferred_element_type=F32)
-        u[:, 256:384] = lax.dot_general(lead[0], own_ref[0], NT, preferred_element_type=F32) + lax.dot_general(lead[1], own_ref[1], NT, preferred_element_type=F32)
+        for k in (8, 0, 1, 2, 3, 4, 5, 6, 7):
+            fetch(k).start()
+
+        def lead(t):
+            return lead_ref[t].reshape(256, 512)
+
+        u[:, 0:256] = product(lead, lead)
+        u[:, 256:384] = product(lead, lambda t: own_ref[t])
         balance(u)
-
-    for part_at in range(8):
-        @pl.when(step == part_at)
+        eliminate(u, 0)
+        fetch(8).wait()
+        tile(0)
+
+    for k in range(1, 8):
+        @pl.when(step == k)
         def _():
-            tile()
-            eliminate(u, part_at)
+            tile(k)
+            eliminate(u, k)
 
     @pl.when(step == 7)
     def _():
@@ -639,6 +650,7 @@
 
 def gram_and_panel(rows, cols, lead, own):
     width, half = rows.shape[2:]
+    hbm = pl.BlockSpec(memory_space=pl.ANY)
     return pl.pallas_call(
         gram_kernel,
         grid=(8,),
@@ -647,8 +659,8 @@
             jax.ShapeDtypeStruct((width, width), F32),
         ),
         in_specs=[
-            pl.BlockSpec((2, 2, width, half), lambda s: (0, s, 0, 0)),
-            pl.BlockSpec((2, 4, width, half), lambda s: (0, 0, 0, 0)),
+            hbm,
+            hbm,
             pl.BlockSpec((2, 2, width, half), lambda s: (0, 0, 0, 0)),
             pl.BlockSpec((2, width, half), lambda s: (0, 0, 0)),
         ],
@@ -656,7 +668,12 @@
             pl.BlockSpec((4, 2 * width, width), lambda s: (0, s, 0)),
             pl.BlockSpec((width, width), lambda s: (0, 0)),
         ),
-        scratch_shapes=[pltpu.VMEM((PANEL, 384), F32), pltpu.VMEM((8, 128), F32)],
+        scratch_shapes=[
+            pltpu.VMEM((PANEL, 384), F32),
+            pltpu.VMEM((2, 16, width, half), jnp.bfloat16),
+            pltpu.VMEM((2, 4, width, half), jnp.bfloat16),
+            pltpu.SemaphoreType.DMA((9,)),
+        ],
         compiler_params=pltpu.CompilerParams(vmem_limit_bytes=60 * 2**20),
         cost_estimate=pl.CostEstimate(flops=2 * 2048 * 512 * 1024, bytes_accessed=10 * 2**20, transcendentals=0),
     )(rows, cols, lead, own)

time: 93 us -> 92.2 us (level)
    pallas_call x1, Pallas kernels: 79.6 us -> 78.1 us  [gather(): pl.pallas_call(gather_kernel, out_shape=(jax.ShapeDtypeStruct((2, 16, wid...]
where the time goes in v3:
time: 92.2 us; the launch traced here: 92.1 us
  Pallas kernels  91.3 us (99%)
    pallas_call x1, Pallas kernels, gather(): pl.pallas_call(gather_kernel, out_shape=(jax.ShapeDtypeStruct((2, 16, wid...  78.1 us
    pallas_call x1, Pallas kernels, gram_and_panel(): pl.pallas_call(gram_kernel, grid=(8,), out_shape=(jax.ShapeDtypeStruct((4...  13.2 us

profile of v3, /device:TPU:27, one launch (start us, length us, event | category | flops | bytes accessed | tf_op | source)
XLA Modules:
  0.0 92.1 jit_solution(17371124969962544813)
XLA Ops:
  0.6 78.1 %shard_map.50 = (bf16[2,16,128,512]{3,2,1,0:T(8,128)(2,1)}, bf16[2,4,128,512]{3,2,1,0:T(8,128)(2,1)}, bf16[2,2,128,512]{3,2,1,0:T(8,128)(2,1)}, bf16[2,128,512]{2,1,0:T(8,128)(2,1)}) custom-call(bf16[512,512]{1,0:T(8,128)(2,1)} %tokens_hbm.1, bf16[8192,128]{1,0:T(8,128)(2,1)} %gate_hbm.1, bf16[8192,128]{1,0:T(8,128)(2,1)} %up_hbm.1), custom_call_target="tpu_custom_call" | custom-call | flops 2147483648 | bytes 12582912 | tf_op jit(solution)/shard_map/pallas_call | solution.py:572
  78.7 13.2 %shard_map.51 = (f32[4,2048,128]{2,1,0:T(8,128)}, f32[128,128]{1,0:T(8,128)}) custom-call(bf16[2,16,128,512]{3,2,1,0:T(8,128)(2,1)} %get-tuple-element.8.rows_hbm, bf16[2,4,128,512]{3,2,1,0:T(8,128)(2,1)} %get-tuple-element.9.cols_hbm, bf16[2,2,128,512]{3,2,1,0:T(8,128)(2,1)} %get-tuple-element.10.lead_ref, bf16[2,128,512]{2,1,0:T(8,128)(2,1)} %get-tuple-element.11.own_ref), custom_call_target="tpu_custom_call" | custom-call | flops 2147483648 | bytes 10485760 | tf_op jit(solution)/shard_map/pallas_call | solution.py:654

commit v4 on v3

--- a/solution.py
+++ b/solution.py
@@ -20,7 +20,7 @@
 FIRST_Z = (352, 160)
 PIECES = 4
 BATCHES = (2, 2, 2, 2, 2, 2, 1, 1, 1)
-RATE, HOP, ISSUE, AHEAD = 49.0, 2.0, 0.12, 0.5
+RATE, HOP, ISSUE, AHEAD = 49.0, 2.0, 0.14, 0.5
 
 
 class Move:
@@ -94,24 +94,21 @@
             add("xp%s%d" % (sign, p), "x" + sign, piece, ["zl%d" % p], ("cols", (0, "other"), (-d, "other"), "x" + sign, p))
         add("xr+%d" % p, "x+", piece, ["xo+%d" % p, "xp+%d" % p], ("cols", (-1, 0), (2, 0), "x+", p))
     add("xr-", "x-", block, ["x%s-%d" % (k, p) for k in "op" for p in every], ("cols", (1, 1), (2, 1), "x-", None))
-    gone = {0: ([], []), -1: (["za+"], ["zb+"]), 1: (["za-"], ["zb-"]), 2: (["zr+"], ["zr-"])}
+    gone = {0: [], -1: ["z+"], 1: ["z-"], 2: ["zr+", "zr-"]}
     for relayed, (sign, d) in enumerate((("+", 1), ("-", -1))):
         link = "u" if d == 1 else "d"
-        for which, half in enumerate("ab"):
-            add("z" + half + sign, link, block, [], ("rows", (0, 0), (-d, 0), "z" + sign, which))
-            for h in OFFSETS:
-                add("y%d" % h + half + sign, "y" + sign, block // 2, gone[h][which], ("rows", (h, 0), (h, -d), "y" + sign, which))
-        add("zr" + sign, link, block, ["z" + "ab"[relayed] + sign], ("rows", (-d, 0), (2, 0), "z" + sign, relayed))
+        add("z" + sign, link, 2 * block, [], ("rows", (0, 0), (-d, 0), "z" + sign, None))
+        add("zr" + sign, link, block, ["z" + sign], ("rows", (-d, 0), (2, 0), "z" + sign, relayed))
         for h in OFFSETS:
-            need = ["y%d" % h + "ab"[relayed] + sign]
-            add("y%dr" % h + sign, "y" + sign, block // 2, need, ("rows", (h, -d), (h, 2), "y" + sign, relayed))
+            add("y%d" % h + sign, "y" + sign, block, gone[h], ("rows", (h, 0), (h, -d), "y" + sign, None))
+            add("y%dr" % h + sign, "y" + sign, block // 2, ["y%d" % h + sign], ("rows", (h, -d), (h, 2), "y" + sign, relayed))
     for p in every:
         first = [name % p for name in ("zl%d", "xo+%d", "xo-%d", "xp+%d", "xp-%d", "xr+%d")]
         for hop in (1, 2, 3):
             add("c%d%d" % (hop, p), "c%d" % hop, piece, first if hop == 1 else ["c%d%d" % (hop - 1, p)], ("chain", hop, p))
         add("l%d" % p, "l", piece, ["c3%d" % p], ("spread", p))
         add("m%d" % p, "m", piece, ["l%d" % p], ("relay", p))
-    row_groups = {h: gone[h][0] + gone[h][1] + ["y%d" % h + k + sign for k in "abr" for sign in "+-"] for h in OFFSETS}
+    row_groups = {h: gone[h] + ["y%d" % h + k + sign for k in ("", "r") for sign in "+-"] for h in OFFSETS}
     pairs = {0: ["zl%d" % p for p in every], 2: ["xr-"] + ["xr+%d" % p for p in every]}
     for sign, d in (("+", -1), ("-", 1)):
         pairs[d] = ["x%s%s%d" % (k, sign, p) for k in "op" for p in every]
@@ -168,7 +165,7 @@
     u[:, PANEL:] = u[:, PANEL:] * down
 
 
-def eliminate(u, piece):
+def eliminate(u, piece, beside):
     wide = lax.broadcasted_iota(jnp.int32, (8, 384), 0)
     base = 64 * (piece // 2)
     groups = [u[base + 8 * g:base + 8 * g + 8, :] for g in range(8)]
@@ -212,6 +209,7 @@
             for k in range(8):
                 acc = acc - thrice(cols[g, k]) * lines[k]
             groups[g] = acc
+        beside(p % 4)
     for g in range(4 * (piece % 2), 8):
         u[base + 8 * g:base + 8 * g + 8, :] = groups[g]
     if piece % 2 and piece < 7:
@@ -590,7 +588,7 @@
             pltpu.SemaphoreType.DMA((1,)),
             pltpu.SemaphoreType.DMA((120,)),
             pltpu.SemaphoreType.DMA((1,)),
-            pltpu.SemaphoreType.DMA((55,)),
+            pltpu.SemaphoreType.DMA((45,)),
             pltpu.SemaphoreType.DMA((10,)),
             pltpu.SemaphoreType.DMA((10,)),
             pltpu.SemaphoreType.DMA((4 * PIECES,)),
@@ -604,44 +602,34 @@
     )(tokens, gate_weight, up_weight)
 
 
-def gram_kernel(rows_hbm, cols_hbm, lead_ref, own_ref, gram_ref, panel_ref, u, rows, cols, sems):
+def gram_kernel(rows_ref, cols_ref, lead_ref, own_ref, gram_ref, panel_ref, u):
     step = pl.program_id(0)
-
-    def fetch(k):
-        if k == 8:
-            return pltpu.make_async_copy(cols_hbm, cols, sems.at[8])
-        pair = pl.ds(2 * k, 2)
-        return pltpu.make_async_copy(rows_hbm.at[:, pair], rows.at[:, pair], sems.at[k])
 
     def product(left, right):
         return sum(lax.dot_general(left(t), right(t), NT, preferred_element_type=F32) for t in (0, 1))
 
-    def tile(k):
-        fetch(k).wait()
-        whole = product(lambda t: rows[t, 2 * k:2 * k + 2].reshape(256, 512), lambda t: cols[t].reshape(512, 512))
-        for a in range(4):
-            gram_ref[a] = whole[:, 128 * a:128 * a + 128]
+    def tile(panel):
+        if panel % 2:
+            return
+        whole = product(
+            lambda t: rows_ref[t].reshape(256, 512), lambda t: cols_ref[t, panel:panel + 2].reshape(256, 512)
+        )
+        for a in (0, 1):
+            gram_ref[panel + a] = whole[:, 128 * a:128 * a + 128]
 
     @pl.when(step == 0)
     def _():
-        for k in (8, 0, 1, 2, 3, 4, 5, 6, 7):
-            fetch(k).start()
-
         def lead(t):
             return lead_ref[t].reshape(256, 512)
 
         u[:, 0:256] = product(lead, lead)
         u[:, 256:384] = product(lead, lambda t: own_ref[t])
         balance(u)
-        eliminate(u, 0)
-        fetch(8).wait()
-        tile(0)
-
-    for k in range(1, 8):
+
+    for k in range(8):
         @pl.when(step == k)
         def _():
-            tile(k)
-            eliminate(u, k)
+            eliminate(u, k, tile)
 
     @pl.when(step == 7)
     def _():
@@ -650,7 +638,6 @@
 
 def gram_and_panel(rows, cols, lead, own):
     width, half = rows.shape[2:]
-    hbm = pl.BlockSpec(memory_space=pl.ANY)
     return pl.pallas_call(
         gram_kernel,
         grid=(8,),
@@ -659,8 +646,8 @@
             jax.ShapeDtypeStruct((width, width), F32),
         ),
         in_specs=[
-            hbm,
-            hbm,
+            pl.BlockSpec((2, 2, width, half), lambda s: (0, s, 0, 0)),
+            pl.BlockSpec((2, 4, width, half), lambda s: (0, 0, 0, 0)),
             pl.BlockSpec((2, 2, width, half), lambda s: (0, 0, 0, 0)),
             pl.BlockSpec((2, width, half), lambda s: (0, 0, 0)),
         ],
@@ -668,12 +655,7 @@
             pl.BlockSpec((4, 2 * width, width), lambda s: (0, s, 0)),
             pl.BlockSpec((width, width), lambda s: (0, 0)),
         ),
-        scratch_shapes=[
-            pltpu.VMEM((PANEL, 384), F32),
-            pltpu.VMEM((2, 16, width, half), jnp.bfloat16),
-            pltpu.VMEM((2, 4, width, half), jnp.bfloat16),
-            pltpu.SemaphoreType.DMA((9,)),
-        ],
+        scratch_shapes=[pltpu.VMEM((PANEL, 384), F32)],
         compiler_params=pltpu.CompilerParams(vmem_limit_bytes=60 * 2**20),
         cost_estimate=pl.CostEstimate(flops=2 * 2048 * 512 * 1024, bytes_accessed=10 * 2**20, transcendentals=0),
     )(rows, cols, lead, own)

time: 92.2 us -> 94.2 us (1.022)
  Pallas kernels: 91.3 us -> 92.6 us
    pallas_call x1, Pallas kernels: 78.1 us -> 80.1 us  [gather(): pl.pallas_call(gather_kernel, out_shape=(jax.ShapeDtypeStruct((2, 16, wid...]
where the time goes in v4:
time: 94.2 us; the launch traced here: 93.3 us
  Pallas kernels  92.6 us (98%)
    pallas_call x1, Pallas kernels, gather(): pl.pallas_call(gather_kernel, out_shape=(jax.ShapeDtypeStruct((2, 16, wid...  80.1 us
    pallas_call x1, Pallas kernels, gram_and_panel(): pl.pallas_call(gram_kernel, grid=(8,), out_shape=(jax.ShapeDtypeStruct((4...  12.5 us

profile of v4, /device:TPU:27, one launch (start us, length us, event | category | flops | bytes accessed | tf_op | source)
XLA Modules:
  0.0 93.3 jit_solution(14782818013110916998)
XLA Ops:
  0.6 80.1 %shard_map.50 = (bf16[2,16,128,512]{3,2,1,0:T(8,128)(2,1)}, bf16[2,4,128,512]{3,2,1,0:T(8,128)(2,1)}, bf16[2,2,128,512]{3,2,1,0:T(8,128)(2,1)}, bf16[2,128,512]{2,1,0:T(8,128)(2,1)}) custom-call(bf16[512,512]{1,0:T(8,128)(2,1)} %tokens_hbm.1, bf16[8192,128]{1,0:T(8,128)(2,1)} %gate_hbm.1, bf16[8192,128]{1,0:T(8,128)(2,1)} %up_hbm.1), custom_call_target="tpu_custom_call" | custom-call | flops 2147483648 | bytes 12582912 | tf_op jit(solution)/shard_map/pallas_call | solution.py:570
  80.7 12.5 %shard_map.51 = (f32[4,2048,128]{2,1,0:T(8,128)}, f32[128,128]{1,0:T(8,128)}) custom-call(bf16[2,16,128,512]{3,2,1,0:T(8,128)(2,1)} %get-tuple-element.8.rows_ref, bf16[2,4,128,512]{3,2,1,0:T(8,128)(2,1)} %get-tuple-element.9.cols_ref, bf16[2,2,128,512]{3,2,1,0:T(8,128)(2,1)} %get-tuple-element.10.lead_ref, bf16[2,128,512]{2,1,0:T(8,128)(2,1)} %get-tuple-element.11.own_ref), custom_call_target="tpu_custom_call" | custom-call | flops 2147483648 | bytes 10485760 | tf_op jit(solution)/shard_map/pallas_call | solution.py:641

commit v5 on v3

--- a/solution.py
+++ b/solution.py
@@ -186,7 +186,8 @@
         }
         for k in range(0, 8, 2):
             a, b, c = spread(cols[p, k], k), spread(cols[p, k + 1], k), spread(cols[p, k + 1], k + 1)
-            over = 1.0 / (a * c - b * b)
+            root = lax.rsqrt(a * c - b * b)
+            over = root * root
             left, right = [], []
             for g in range(p, 8):
                 left.append((c * cols[g, k] - b * cols[g, k + 1]) * over)
@@ -423,7 +424,8 @@
         source, target = side_refs(kind, d)
         if kind != "c":
             side(index, source, target(tok)).start()
-            keep(index, source, target(tok)).start()
+            if kind != "r":
+                keep(index, source, target(tok)).start()
             return
 
         @pl.when(keeps[d])
@@ -439,7 +441,8 @@
         if kind != "c":
             side(index, target(1 - tok), target(1 - tok)).wait_recv()
             side(index, source, target(tok)).wait_send()
-            keep(index, source, target(tok)).wait()
+            if kind != "r":
+                keep(index, source, target(tok)).wait()
             return
 
         @pl.when(keeps[d])
@@ -536,6 +539,8 @@
             arrive(hiddens, name, parity)
 
     both(hidden_stage)
+    keep_rows = keep(0, rows, rows_out.at[tok])
+    keep_rows.start()
     held_lead = pltpu.make_async_copy(cols.at[0], leads.at[lax.rem(y, 2)], local_sem.at[10])
 
     @pl.when(at_z[0])
@@ -558,6 +563,7 @@
     gone = weights.at[pl.ds(0, 5632), :]
     remote((send2, recv2), 0, gone, gone, sibling).wait_send()
     both(lead_end)
+    keep_rows.wait()
     for kind, d in shared:
         side_end(kind, d, shared[kind, d][1])
     side_end("o", 0, 8)
@@ -604,43 +610,30 @@
     )(tokens, gate_weight, up_weight)
 
 
-def gram_kernel(rows_hbm, cols_hbm, lead_ref, own_ref, gram_ref, panel_ref, u, rows, cols, sems):
+def gram_kernel(rows_ref, cols_ref, lead_ref, own_ref, gram_ref, panel_ref, u):
     step = pl.program_id(0)
-
-    def fetch(k):
-        if k == 8:
-            return pltpu.make_async_copy(cols_hbm, cols, sems.at[8])
-        pair = pl.ds(2 * k, 2)
-        return pltpu.make_async_copy(rows_hbm.at[:, pair], rows.at[:, pair], sems.at[k])
 
     def product(left, right):
         return sum(lax.dot_general(left(t), right(t), NT, preferred_element_type=F32) for t in (0, 1))
 
-    def tile(k):
-        fetch(k).wait()
-        whole = product(lambda t: rows[t, 2 * k:2 * k + 2].reshape(256, 512), lambda t: cols[t].reshape(512, 512))
+    def tile():
+        whole = product(lambda t: rows_ref[t].reshape(256, 512), lambda t: cols_ref[t].reshape(512, 512))
         for a in range(4):
             gram_ref[a] = whole[:, 128 * a:128 * a + 128]
 
     @pl.when(step == 0)
     def _():
-        for k in (8, 0, 1, 2, 3, 4, 5, 6, 7):
-            fetch(k).start()
-
         def lead(t):
             return lead_ref[t].reshape(256, 512)
 
         u[:, 0:256] = product(lead, lead)
         u[:, 256:384] = product(lead, lambda t: own_ref[t])
         balance(u)
-        eliminate(u, 0)
-        fetch(8).wait()
-        tile(0)
-
-    for k in range(1, 8):
+
+    for k in range(8):
         @pl.when(step == k)
         def _():
-            tile(k)
+            tile()
             eliminate(u, k)
 
     @pl.when(step == 7)
@@ -650,7 +643,6 @@
 
 def gram_and_panel(rows, cols, lead, own):
     width, half = rows.shape[2:]
-    hbm = pl.BlockSpec(memory_space=pl.ANY)
     return pl.pallas_call(
         gram_kernel,
         grid=(8,),
@@ -659,8 +651,8 @@
             jax.ShapeDtypeStruct((width, width), F32),
         ),
         in_specs=[
-            hbm,
-            hbm,
+            pl.BlockSpec((2, 2, width, half), lambda s: (0, s, 0, 0)),
+            pl.BlockSpec((2, 4, width, half), lambda s: (0, 0, 0, 0)),
             pl.BlockSpec((2, 2, width, half), lambda s: (0, 0, 0, 0)),
             pl.BlockSpec((2, width, half), lambda s: (0, 0, 0)),
         ],
@@ -668,12 +660,7 @@
             pl.BlockSpec((4, 2 * width, width), lambda s: (0, s, 0)),
             pl.BlockSpec((width, width), lambda s: (0, 0)),
         ),
-        scratch_shapes=[
-            pltpu.VMEM((PANEL, 384), F32),
-            pltpu.VMEM((2, 16, width, half), jnp.bfloat16),
-            pltpu.VMEM((2, 4, width, half), jnp.bfloat16),
-            pltpu.SemaphoreType.DMA((9,)),
-        ],
+        scratch_shapes=[pltpu.VMEM((PANEL, 384), F32)],
         compiler_params=pltpu.CompilerParams(vmem_limit_bytes=60 * 2**20),
         cost_estimate=pl.CostEstimate(flops=2 * 2048 * 512 * 1024, bytes_accessed=10 * 2**20, transcendentals=0),
     )(rows, cols, lead, own)

time: 92.2 us -> 91.6 us (level)
  no operation moved by 1% of the time
where the time goes in v5:
time: 91.6 us; the launch traced here: 91.3 us
  Pallas kernels  90.7 us (99%)
    pallas_call x1, Pallas kernels, gather(): pl.pallas_call(gather_kernel, out_shape=(jax.ShapeDtypeStruct((2, 16, wid...  78.1 us
    pallas_call x1, Pallas kernels, gram_and_panel(): pl.pallas_call(gram_kernel, grid=(8,), out_shape=(jax.ShapeDtypeStruct((4...  12.6 us

profile of v5, /device:TPU:27, one launch (start us, length us, event | category | flops | bytes accessed | tf_op | source)
XLA Modules:
  0.0 91.3 jit_solution(9026420941079685306)
XLA Ops:
  0.6 78.1 %shard_map.50 = (bf16[2,16,128,512]{3,2,1,0:T(8,128)(2,1)}, bf16[2,4,128,512]{3,2,1,0:T(8,128)(2,1)}, bf16[2,2,128,512]{3,2,1,0:T(8,128)(2,1)}, bf16[2,128,512]{2,1,0:T(8,128)(2,1)}) custom-call(bf16[512,512]{1,0:T(8,128)(2,1)} %tokens_hbm.1, bf16[8192,128]{1,0:T(8,128)(2,1)} %gate_hbm.1, bf16[8192,128]{1,0:T(8,128)(2,1)} %up_hbm.1), custom_call_target="tpu_custom_call" | custom-call | flops 2147483648 | bytes 12582912 | tf_op jit(solution)/shard_map/pallas_call | solution.py:578
  78.7 12.6 %shard_map.51 = (f32[4,2048,128]{2,1,0:T(8,128)}, f32[128,128]{1,0:T(8,128)}) custom-call(bf16[2,16,128,512]{3,2,1,0:T(8,128)(2,1)} %get-tuple-element.8.rows_ref, bf16[2,4,128,512]{3,2,1,0:T(8,128)(2,1)} %get-tuple-element.9.cols_ref, bf16[2,2,128,512]{3,2,1,0:T(8,128)(2,1)} %get-tuple-element.10.lead_ref, bf16[2,128,512]{2,1,0:T(8,128)(2,1)} %get-tuple-element.11.own_ref), custom_call_target="tpu_custom_call" | custom-call | flops 2147483648 | bytes 10485760 | tf_op jit(solution)/shard_map/pallas_call | solution.py:646

commit v6 on v5

--- a/solution.py
+++ b/solution.py
@@ -20,7 +20,7 @@
 FIRST_Z = (352, 160)
 PIECES = 4
 BATCHES = (2, 2, 2, 2, 2, 2, 1, 1, 1)
-RATE, HOP, ISSUE, AHEAD = 49.0, 2.0, 0.12, 0.5
+RATE, HOP, ISSUE, AHEAD = 49.0, 2.3, 0.14, 1.5
 
 
 class Move:
@@ -170,8 +170,8 @@
 
 def eliminate(u, piece):
     wide = lax.broadcasted_iota(jnp.int32, (8, 384), 0)
-    base = 64 * (piece // 2)
-    groups = [u[base + 8 * g:base + 8 * g + 8, :] for g in range(8)]
+    base = 32 * piece
+    groups = [u[base + 8 * g:base + 8 * g + 8, :] for g in range(4)]
 
     def spread(row, at):
         return jnp.broadcast_to(row[at:at + 1, :], (8, row.shape[1]))
@@ -179,22 +179,22 @@
     def thrice(tile):
         return jnp.concatenate([tile] * 3, axis=1)
 
-    for p in range(4 * (piece % 2), 4 * (piece % 2) + 4):
+    for p in range(4):
         cols = {
             (g, k): jnp.broadcast_to(groups[g][:, base + 8 * p + k:base + 8 * p + k + 1], (8, 128))
-            for g in range(p, 8) for k in range(8)
+            for g in range(p, 4) for k in range(8)
         }
         for k in range(0, 8, 2):
             a, b, c = spread(cols[p, k], k), spread(cols[p, k + 1], k), spread(cols[p, k + 1], k + 1)
             root = lax.rsqrt(a * c - b * b)
             over = root * root
             left, right = [], []
-            for g in range(p, 8):
+            for g in range(p, 4):
                 left.append((c * cols[g, k] - b * cols[g, k + 1]) * over)
                 right.append((a * cols[g, k + 1] - b * cols[g, k]) * over)
             for j in range(k + 2, 8):
                 one, two = spread(cols[p, k], j), spread(cols[p, k + 1], j)
-                for g in range(p, 8):
+                for g in range(p, 4):
                     cols[g, j] = cols[g, j] - (left[g - p] * one + right[g - p] * two)
             first = lax.rsqrt(a)
             ratio = b * first * first
@@ -204,22 +204,22 @@
             low = (below - thrice(ratio) * line) * thrice(second)
             rest = groups[p] - (thrice(left[0]) * line + thrice(right[0]) * below)
             groups[p] = jnp.where(wide == k, top, jnp.where(wide == k + 1, low, jnp.where(wide > k + 1, rest, groups[p])))
-            for g in range(p, 8):
+            for g in range(p, 4):
                 cols[g, k + 1] = (cols[g, k + 1] - ratio * cols[g, k]) * second
                 cols[g, k] = cols[g, k] * first
         lines = [spread(groups[p], k) for k in range(8)]
-        for g in range(p + 1, 8):
+        for g in range(p + 1, 4):
             acc = groups[g]
             for k in range(8):
                 acc = acc - thrice(cols[g, k]) * lines[k]
             groups[g] = acc
-    for g in range(4 * (piece % 2), 8):
+    for g in range(4):
         u[base + 8 * g:base + 8 * g + 8, :] = groups[g]
-    if piece % 2 and piece < 7:
-        block = u[base:base + 64, :]
-        first = 0 if base == 0 else 128
+    if piece < 7:
+        block = u[base:base + 32, :]
+        first = 0 if piece < 3 else 128
         update = jnp.dot(block[:, first:256].T, block, precision=HIGH, preferred_element_type=F32)
-        rest = base + 64
+        rest = base + 32
         u[rest:256, :] = u[rest:256, :] - update[rest - first:256 - first, :]
 
 

time: 91.6 us -> 92.7 us (1.012)
  no operation moved by 1% of the time
where the time goes in v6:
time: 92.7 us; the launch traced here: 91.8 us
  Pallas kernels  91.1 us (98%)
    pallas_call x1, Pallas kernels, gather(): pl.pallas_call(gather_kernel, out_shape=(jax.ShapeDtypeStruct((2, 16, wid...  77.8 us
    pallas_call x1, Pallas kernels, gram_and_panel(): pl.pallas_call(gram_kernel, grid=(8,), out_shape=(jax.ShapeDtypeStruct((4...  13.4 us

profile of v6, /device:TPU:27, one launch (start us, length us, event | category | flops | bytes accessed | tf_op | source)
XLA Modules:
  0.0 91.8 jit_solution(13872734455289086766)
XLA Ops:
  0.6 77.8 %shard_map.50 = (bf16[2,16,128,512]{3,2,1,0:T(8,128)(2,1)}, bf16[2,4,128,512]{3,2,1,0:T(8,128)(2,1)}, bf16[2,2,128,512]{3,2,1,0:T(8,128)(2,1)}, bf16[2,128,512]{2,1,0:T(8,128)(2,1)}) custom-call(bf16[512,512]{1,0:T(8,128)(2,1)} %tokens_hbm.1, bf16[8192,128]{1,0:T(8,128)(2,1)} %gate_hbm.1, bf16[8192,128]{1,0:T(8,128)(2,1)} %up_hbm.1), custom_call_target="tpu_custom_call" | custom-call | flops 2147483648 | bytes 12582912 | tf_op jit(solution)/shard_map/pallas_call | solution.py:578
  78.4 13.4 %shard_map.51 = (f32[4,2048,128]{2,1,0:T(8,128)}, f32[128,128]{1,0:T(8,128)}) custom-call(bf16[2,16,128,512]{3,2,1,0:T(8,128)(2,1)} %get-tuple-element.8.rows_ref, bf16[2,4,128,512]{3,2,1,0:T(8,128)(2,1)} %get-tuple-element.9.cols_ref, bf16[2,2,128,512]{3,2,1,0:T(8,128)(2,1)} %get-tuple-element.10.lead_ref, bf16[2,128,512]{2,1,0:T(8,128)(2,1)} %get-tuple-element.11.own_ref), custom_call_target="tpu_custom_call" | custom-call | flops 2147483648 | bytes 10485760 | tf_op jit(solution)/shard_map/pallas_call | solution.py:646

commit v7 on v5

--- a/solution.py
+++ b/solution.py
@@ -20,7 +20,7 @@
 FIRST_Z = (352, 160)
 PIECES = 4
 BATCHES = (2, 2, 2, 2, 2, 2, 1, 1, 1)
-RATE, HOP, ISSUE, AHEAD = 49.0, 2.0, 0.12, 0.5
+RATE, HOP, ISSUE, AHEAD = 49.0, 2.3, 0.14, 1.5
 
 
 class Move:

time: 91.6 us -> 92 us (level)
  no operation moved by 1% of the time
where the time goes in v7:
time: 92 us; the launch traced here: 91 us
  Pallas kernels  90.4 us (98%)
    pallas_call x1, Pallas kernels, gather(): pl.pallas_call(gather_kernel, out_shape=(jax.ShapeDtypeStruct((2, 16, wid...  77.8 us
    pallas_call x1, Pallas kernels, gram_and_panel(): pl.pallas_call(gram_kernel, grid=(8,), out_shape=(jax.ShapeDtypeStruct((4...  12.6 us

profile of v7, /device:TPU:27, one launch (start us, length us, event | category | flops | bytes accessed | tf_op | source)
XLA Modules:
  0.0 91.0 jit_solution(15818648178823087799)
XLA Ops:
  0.6 77.8 %shard_map.50 = (bf16[2,16,128,512]{3,2,1,0:T(8,128)(2,1)}, bf16[2,4,128,512]{3,2,1,0:T(8,128)(2,1)}, bf16[2,2,128,512]{3,2,1,0:T(8,128)(2,1)}, bf16[2,128,512]{2,1,0:T(8,128)(2,1)}) custom-call(bf16[512,512]{1,0:T(8,128)(2,1)} %tokens_hbm.1, bf16[8192,128]{1,0:T(8,128)(2,1)} %gate_hbm.1, bf16[8192,128]{1,0:T(8,128)(2,1)} %up_hbm.1), custom_call_target="tpu_custom_call" | custom-call | flops 2147483648 | bytes 12582912 | tf_op jit(solution)/shard_map/pallas_call | solution.py:578
  78.4 12.6 %shard_map.51 = (f32[4,2048,128]{2,1,0:T(8,128)}, f32[128,128]{1,0:T(8,128)}) custom-call(bf16[2,16,128,512]{3,2,1,0:T(8,128)(2,1)} %get-tuple-element.8.rows_ref, bf16[2,4,128,512]{3,2,1,0:T(8,128)(2,1)} %get-tuple-element.9.cols_ref, bf16[2,2,128,512]{3,2,1,0:T(8,128)(2,1)} %get-tuple-element.10.lead_ref, bf16[2,128,512]{2,1,0:T(8,128)(2,1)} %get-tuple-element.11.own_ref), custom_call_target="tpu_custom_call" | custom-call | flops 2147483648 | bytes 10485760 | tf_op jit(solution)/shard_map/pallas_call | solution.py:646
